TPU v7x, 32 devices: a whole 2x2x4 slice. The times are simulated.
32 devices in a mesh: rep: 16 (over z, x, core), shard: 2 (over y).
Axes of the slice: x: 2, y: 2, z: 4, core: 2. Of those that a mesh axis runs over, the one named last changes fastest.
Arguments:
- tokens: bfloat16 [4096, 1024], P(('rep', 'shard')), may hold values from -6 to 6
- cotangent: bfloat16 [4096, 1024], P(('rep', 'shard')), may hold values from -6 to 6
- segment_ids: int32 [4096], P(('rep', 'shard')), may hold values from -1 to 7, as said below
- flat_weights: float32 [12595200], P('shard')
- first_moment: float32 [12595200], P('shard'), may hold values from -1.2 to 1.2
- second_moment: float32 [12595200], P('shard'), may hold values from 0.5 to 2
Outputs:
- output: bfloat16 [4096, 1024], P(('rep', 'shard'))
- input_grad: bfloat16 [4096, 1024], P(('rep', 'shard'))
- weight_grad: float32 [12595200], P('shard')
- new_weights: float32 [12595200], P('shard')
- new_first: float32 [12595200], P('shard')
- new_second: float32 [12595200], P('shard')
Inputs may be any that keep to these rules, and one draw needn't show every extreme that they name: `segment_ids`: within each device's 128 rows the live rows come first, numbered 0, 1, 2 ... by sequence and never falling, followed by padding rows of -1; every sequence and every live span is a multiple of 16 rows, and each device has at least a quarter of its rows live. In every draw some device's rows form a single sequence of 128 rows, and some device has 8 sequences.
All inputs are finite; a program needn't handle non-finite values.
Results may differ from a plain program's by a relative error of at most 0.012.
The roundings to bfloat16 on the way count: a program that leaves them out, or rounds other values in their place, can miss the bound.
Values may be sent and summed in bfloat16 or wider, within the bound.
A program may use at most 512 MiB of HBM per device.

v0:
```python
import math
import jax
import jax.numpy as jnp
from jax import lax
from jax.sharding import PartitionSpec as P

D = 1024
HEADS = 16
HD = 64
FF = 4096
STEP = 3


def shapes_list():
    width = HEADS * HD
    return [
        (D, width),
        (D, width),
        (D, width),
        (width, D),
        (D, FF),
        (FF, D),
        (width,),
        (width,),
        (D,),
        (D,),
        (D,),
        (FF,),
        (D,),
        (D,),
        (D,),
    ]


def unpack(flat_vec):
    pieces = []
    offset = 0
    for extent in shapes_list():
        amount = math.prod(extent)
        pieces.append(lax.slice_in_dim(flat_vec, offset, offset + amount).reshape(extent))
        offset = offset + amount
    return pieces


def layer_norm(values, gain, shift):
    center = values - jnp.mean(values, axis=1, keepdims=True)
    spread = lax.rsqrt(jnp.mean(center * center, axis=1, keepdims=True) + 1e-05)
    normed = center * spread
    return (normed * gain.astype(jnp.float32) + shift.astype(jnp.float32), normed, spread)


def norm_back(upstream, normed, spread, gain):
    scaled = upstream * gain.astype(jnp.float32)
    inner = (
        scaled
        - jnp.mean(scaled, axis=1, keepdims=True)
        - normed * jnp.mean(scaled * normed, axis=1, keepdims=True)
    )
    return (spread * inner, jnp.sum(upstream * normed, axis=0), jnp.sum(upstream, axis=0))


def gelu_pair(values):
    cdf_part = 0.5 * (1.0 + lax.erf(values * 0.5**0.5))
    density = jnp.exp(-0.5 * values * values) * (2.0 * math.pi) ** (-0.5)
    return (values * cdf_part, cdf_part + values * density)


def heads_of(matrix):
    return matrix.reshape(matrix.shape[0], HEADS, HD)


def scores_of(query, keys, allowed):
    raw = jnp.einsum(
        "qhd,khd->hqk", heads_of(query), heads_of(keys), preferred_element_type=jnp.float32
    ) * HD ** (-0.5)
    return jnp.where(allowed[None, :, :], raw, -1e30)


def forward_pass(tokens, segment, params):
    (
        query_weight,
        key_weight,
        value_weight,
        output_weight,
        inner_weight,
        outer_weight,
        query_bias,
        value_bias,
        output_bias,
        first_gain,
        first_shift,
        inner_bias,
        outer_bias,
        second_gain,
        second_shift,
    ) = params
    rows = tokens.shape[0]
    residual = tokens.astype(jnp.float32)
    query = (
        jnp.dot(tokens, query_weight, preferred_element_type=jnp.float32)
        + query_bias.astype(jnp.float32)
    ).astype(jnp.bfloat16)
    keys = jnp.dot(tokens, key_weight, preferred_element_type=jnp.float32).astype(jnp.bfloat16)
    values = (
        jnp.dot(tokens, value_weight, preferred_element_type=jnp.float32)
        + value_bias.astype(jnp.float32)
    ).astype(jnp.bfloat16)
    allowed = segment[:, None] == segment[None, :]
    scores = scores_of(query, keys, allowed)
    row_max = jnp.max(scores, axis=2, keepdims=True)
    expo = jnp.exp(scores - row_max)
    row_sum = jnp.sum(expo, axis=2, keepdims=True)
    log_sum = row_max + jnp.log(row_sum)
    attn_prob = (expo / row_sum).astype(jnp.bfloat16)
    context = (
        jnp.einsum("hqk,khd->qhd", attn_prob, heads_of(values), preferred_element_type=jnp.float32)
        .reshape(rows, HEADS * HD)
        .astype(jnp.bfloat16)
    )
    attended = jnp.dot(
        context, output_weight, preferred_element_type=jnp.float32
    ) + output_bias.astype(jnp.float32)
    first_norm, first_normed, first_spread = layer_norm(
        residual + attended, first_gain, first_shift
    )
    first_round = first_norm.astype(jnp.bfloat16)
    inner_pre = jnp.dot(
        first_round, inner_weight, preferred_element_type=jnp.float32
    ) + inner_bias.astype(jnp.float32)
    inner_act, inner_slope = gelu_pair(inner_pre)
    inner_round = inner_act.astype(jnp.bfloat16)
    outer = jnp.dot(
        inner_round, outer_weight, preferred_element_type=jnp.float32
    ) + outer_bias.astype(jnp.float32)
    second_norm, second_normed, second_spread = layer_norm(
        first_norm + outer, second_gain, second_shift
    )
    live = (segment >= 0)[:, None]
    output = jnp.where(live, second_norm, residual).astype(jnp.bfloat16)
    saved = (
        query,
        keys,
        values,
        allowed,
        log_sum,
        context,
        first_normed,
        first_spread,
        first_round,
        inner_slope,
        inner_round,
        second_normed,
        second_spread,
        live,
    )
    return (output, saved)


def backward_pass(tokens, cotangent, saved, params):
    (
        query_weight,
        key_weight,
        value_weight,
        output_weight,
        inner_weight,
        outer_weight,
        query_bias,
        value_bias,
        output_bias,
        first_gain,
        first_shift,
        inner_bias,
        outer_bias,
        second_gain,
        second_shift,
    ) = params
    (
        query,
        keys,
        values,
        allowed,
        log_sum,
        context,
        first_normed,
        first_spread,
        first_round,
        inner_slope,
        inner_round,
        second_normed,
        second_spread,
        live,
    ) = saved
    rows = tokens.shape[0]
    upstream = jnp.where(live, cotangent.astype(jnp.float32), 0.0)
    back_second, grad_second_gain, grad_second_shift = norm_back(
        upstream, second_normed, second_spread, second_gain
    )
    back_second_round = back_second.astype(jnp.bfloat16)
    grad_outer_weight = jnp.dot(
        inner_round.T, back_second_round, preferred_element_type=jnp.float32
    )
    grad_outer_bias = jnp.sum(back_second, axis=0)
    back_inner = (
        jnp.dot(back_second_round, outer_weight.T, preferred_element_type=jnp.float32) * inner_slope
    )
    back_inner_round = back_inner.astype(jnp.bfloat16)
    grad_inner_weight = jnp.dot(first_round.T, back_inner_round, preferred_element_type=jnp.float32)
    grad_inner_bias = jnp.sum(back_inner, axis=0)
    back_first_out = back_second + jnp.dot(
        back_inner_round, inner_weight.T, preferred_element_type=jnp.float32
    )
    back_first, grad_first_gain, grad_first_shift = norm_back(
        back_first_out, first_normed, first_spread, first_gain
    )
    back_first_round = back_first.astype(jnp.bfloat16)
    grad_output_weight = jnp.dot(context.T, back_first_round, preferred_element_type=jnp.float32)
    grad_output_bias = jnp.sum(back_first, axis=0)
    back_context = jnp.dot(
        back_first_round, output_weight.T, preferred_element_type=jnp.float32
    ).astype(jnp.bfloat16)
    prob_again = jnp.exp(scores_of(query, keys, allowed) - log_sum)
    prob_round = prob_again.astype(jnp.bfloat16)
    back_values = jnp.einsum(
        "hqk,qhd->khd", prob_round, heads_of(back_context), preferred_element_type=jnp.float32
    ).reshape(rows, HEADS * HD)
    back_prob = jnp.einsum(
        "qhd,khd->hqk", heads_of(back_context), heads_of(values), preferred_element_type=jnp.float32
    )
    delta_rows = jnp.sum(
        heads_of(back_context).astype(jnp.float32) * heads_of(context).astype(jnp.float32), axis=2
    ).T
    back_scores = (prob_again * (back_prob - delta_rows[:, :, None]) * HD ** (-0.5)).astype(
        jnp.bfloat16
    )
    back_query = jnp.einsum(
        "hqk,khd->qhd", back_scores, heads_of(keys), preferred_element_type=jnp.float32
    ).reshape(rows, HEADS * HD)
    back_keys = jnp.einsum(
        "hqk,qhd->khd", back_scores, heads_of(query), preferred_element_type=jnp.float32
    ).reshape(rows, HEADS * HD)
    query_round = back_query.astype(jnp.bfloat16)
    keys_round = back_keys.astype(jnp.bfloat16)
    values_round = back_values.astype(jnp.bfloat16)
    grad_query_weight = jnp.dot(tokens.T, query_round, preferred_element_type=jnp.float32)
    grad_key_weight = jnp.dot(tokens.T, keys_round, preferred_element_type=jnp.float32)
    grad_value_weight = jnp.dot(tokens.T, values_round, preferred_element_type=jnp.float32)
    grad_query_bias = jnp.sum(back_query, axis=0)
    grad_value_bias = jnp.sum(back_values, axis=0)
    back_input = (
        back_first
        + jnp.dot(query_round, query_weight.T, preferred_element_type=jnp.float32)
        + jnp.dot(keys_round, key_weight.T, preferred_element_type=jnp.float32)
        + jnp.dot(values_round, value_weight.T, preferred_element_type=jnp.float32)
    )
    input_grad = jnp.where(live, back_input, cotangent.astype(jnp.float32)).astype(jnp.bfloat16)
    grad_list = [
        grad_query_weight,
        grad_key_weight,
        grad_value_weight,
        grad_output_weight,
        grad_inner_weight,
        grad_outer_weight,
        grad_query_bias,
        grad_value_bias,
        grad_output_bias,
        grad_first_gain,
        grad_first_shift,
        grad_inner_bias,
        grad_outer_bias,
        grad_second_gain,
        grad_second_shift,
    ]
    flat_grad = jnp.concatenate([member.reshape(-1).astype(jnp.bfloat16) for member in grad_list])
    return (input_grad, flat_grad)


def adamw(grad, weights, first, second):
    first_new = 0.9 * first + 0.1 * grad
    second_new = 0.98 * second + 0.02 * grad * grad
    first_hat = first_new / (1.0 - 0.9**STEP)
    second_hat = second_new / (1.0 - 0.98**STEP)
    weights_new = weights - 0.01 * (first_hat / (jnp.sqrt(second_hat) + 1e-06) + 0.01 * weights)
    return (weights_new, first_new, second_new)


def on_device(tokens, cotangent, segment_ids, flat_weights, first_moment, second_moment):
    gathered = lax.all_gather(flat_weights.astype(jnp.bfloat16), "shard", axis=0, tiled=True)
    params = unpack(gathered)
    output, saved = forward_pass(tokens, segment_ids, params)
    input_grad, local_grad = backward_pass(tokens, cotangent, saved, params)
    shards = lax.axis_size("shard")
    owned_len = local_grad.shape[0] // shards
    received = lax.all_to_all(
        local_grad.reshape(shards, owned_len), "shard", split_axis=0, concat_axis=0, tiled=True
    )
    group_part = jnp.sum(received.astype(jnp.float32), axis=0)
    weight_grad = lax.psum(group_part, "rep")
    new_weights, new_first, new_second = adamw(
        weight_grad, flat_weights, first_moment, second_moment
    )
    return (output, input_grad, weight_grad, new_weights, new_first, new_second)


def solution(mesh):
    return jax.shard_map(
        on_device,
        mesh=mesh,
        in_specs=(
            P(("rep", "shard"), None),
            P(("rep", "shard"), None),
            P(("rep", "shard")),
            P("shard"),
            P("shard"),
            P("shard"),
        ),
        out_specs=(
            P(("rep", "shard"), None),
            P(("rep", "shard"), None),
            P("shard"),
            P("shard"),
            P("shard"),
            P("shard"),
        ),
        check_vma=False,
    )
```

profile of v0, /device:TPU:0, one launch (start us, length us, event | category | flops | bytes accessed | tf_op | source)
XLA Modules:
  0.0 2178.3 jit_solution(18369592160568592269)
XLA Ops:
  7.2 14.5 convert_element_type.203
  22.4 298.6 %all-gather.2.cloned.1.call-done = bf16[12595200]{0:T(1024)(128)(2,1)} async-done(((bf16[6297600]{0:T(1024)(128)(2,1)}), bf16[12595200]{0:T(1024)(128)(2,1)}) %all-gather.2.cloned.1.call-update) | async-done | bytes 25190416 | tf_op jit(solution)/shard_map/all_gather | solution.py:287
  321.0 11.4 fusion.43
  332.5 13.3 slice.122
  345.7 13.3 slice.119
  359.0 6.0 fusion.44
  365.0 2.8 slice.106
  367.9 0.8 slice_convert_fusion.2
  369.3 4.3 slice.109
  373.6 2.0 fusion.14
  375.8 4.3 slice.112
  380.1 2.0 convolution_convert_fusion.3
  383.6 2.9 slice.114
  387.4 1.0 slice_convert_fusion
  388.4 4.9 convolution_add_fusion
  393.4 1.5 fusion.49
  395.5 1.0 fusion.40
  396.6 3.5 fusion.50
  400.1 3.0 multiply_reduce_fusion
  403.4 1.5 convolution_convert_fusion.1
  405.0 1.8 copy.40
  406.8 1.2 multiply_reduce_fusion.1
  408.0 1.8 fusion.8
  409.8 1.4 fusion.46
  411.2 2.2 convolution_convert_fusion
  413.4 2.5 fusion.45
  415.9 3.0 convert_bitcast_fusion.2
  418.9 5.9 convert_bitcast_fusion.1
  424.8 4.7 convert_bitcast_fusion
  429.5 0.7 convert_bitcast_fusion.5
  430.2 2.6 copy.45
  432.7 2.2 copy.54
  435.0 1.5 constant_dynamic-update-slice_fusion.13
  436.4 0.7 convert_bitcast_fusion.4
  437.1 2.9 copy.46
  440.1 3.5 copy.55
  444.3 2.6 copy.47
  446.8 3.6 copy.56
  450.4 3.5 copy.57
  454.0 9.6 copy.58
  463.6 9.1 copy.59
  472.8 1.5 constant_dynamic-update-slice_fusion.12
  474.3 3.8 constant_dynamic-update-slice_fusion.11
  478.1 3.2 constant_dynamic-update-slice_fusion.10
  481.3 4.2 constant_dynamic-update-slice_fusion.9
  485.4 0.7 slice-done.5
  486.2 3.6 constant_dynamic-update-slice_fusion.8
  495.0 299.9 %while.1 = (u32[]{:T(128)}, bf16[12595200]{0:T(1024)(128)(2,1)}, bf16[2,1,6297600]{2,1,0:T(2,128)(2,1)}, u32[]{}, u32[]{}) while((u32[]{:T(128)}, bf16[12595200]{0:T(1024)(128)(2,1)}, bf16[2,1,6297600]{2,1,0:T(2,128)(2,1)}, u32[]{}, u32[]{}) %tuple.54), condition=%wide.cond, body=%wide.body.sunk | while | flops 9 | bytes 62976164
  495.0 5.3 dynamic-slice.2
  500.3 144.6 %reshape_dynamic-update-slice_fusion.2 = bf16[2,1,6297600]{2,1,0:T(2,128)(2,1)} fusion(bf16[2,1,6297600]{2,1,0:T(2,128)(2,1)} %get-tuple-element.92, u32[]{:T(128)S(6)} %multiply.58, u32[]{:T(128)S(6)} %multiply.59, bf16[6297600]{0:T(1024)(128)(2,1)S(1)} %dynamic-slice.2), kind=kLoop, calls=%fused_computation.127.clone.1 | loop fusion | bytes 37785608
  644.9 5.3 dynamic-slice.2
  650.3 144.6 %reshape_dynamic-update-slice_fusion.2 = bf16[2,1,6297600]{2,1,0:T(2,128)(2,1)} fusion(bf16[2,1,6297600]{2,1,0:T(2,128)(2,1)} %get-tuple-element.92, u32[]{:T(128)S(6)} %multiply.58, u32[]{:T(128)S(6)} %multiply.59, bf16[6297600]{0:T(1024)(128)(2,1)S(1)} %dynamic-slice.2), kind=kLoop, calls=%fused_computation.127.clone.1 | loop fusion | bytes 37785608
  795.4 188.4 %reduce.3 = bf16[2,6297600]{1,0:T(2,128)(2,1)} reduce(bf16[2,1,6297600]{2,1,0:T(2,128)(2,1)} %get-tuple-element.10, bf16[]{:T(256)} %broadcast.121), dimensions={1}, to_apply=%get-tuple-element.10.reduce_sub_computation | reduce | bytes 50380800 | tf_op jit(solution)/shard_map/all_to_all | solution.py:293
  983.8 44.6 %reshape.208 = bf16[2,2,3148800]{2,1,0:T(2,128)(2,1)} reshape(bf16[2,6297600]{1,0:T(2,128)(2,1)} %reduce.3) | data formatting | bytes 50380800
  1028.4 297.9 %all_to_all.10 = bf16[2,2,3148800]{2,1,0:T(2,128)(2,1)} all-to-all(bf16[2,2,3148800]{2,1,0:T(2,128)(2,1)} %reshape.208), channel_id=1, replica_groups=mesh['rep'=16,'shard'=2] {'shard'}, dimensions={0} | all-to-all | bytes 50380800 | tf_op jit(solution)/shard_map/all_to_all | solution.py:293
  1326.3 56.2 %reshape.209 = bf16[2,1,6297600]{2,1,0:T(2,128)(2,1)} reshape(bf16[2,2,3148800]{2,1,0:T(2,128)(2,1)} %all_to_all.10) | data formatting | bytes 50380800
  1382.5 270.2 %convert_reduce_fusion = f32[6297600]{0:T(1024)} fusion(bf16[2,1,6297600]{2,1,0:T(2,128)(2,1)} %reshape.209), kind=kLoop, calls=%fused_computation | loop fusion | flops 18892800 | bytes 50380800 | tf_op jit(solution)/shard_map/reduce_sum | solution.py:296
  1652.7 1.0 copy-done.9
  1653.7 2.5 convolution_add_fusion.3
  1656.2 2.4 convolution_add_fusion.2
  1658.7 1.5 fusion.12
  1660.3 432.3 %all-reduce.2.cloned.1.call-done = f32[6297600]{0:T(1024)} async-done(((f32[6297600]{0:T(1024)}), f32[6297600]{0:T(1024)}) %all-reduce.2.cloned.1.call-update) | async-done | bytes 25190416 | tf_op jit(solution)/shard_map/psum | solution.py:297
  2092.6 59.4 %multiply_subtract_fusion = (f32[6297600]{0:T(1024)}, f32[6297600]{0:T(1024)}, f32[6297600]{0:T(1024)}) fusion(f32[6297600]{0:T(1024)} %param.9, f32[6297600]{0:T(1024)} %all-reduce.2.cloned.1.call-done, f32[6297600]{0:T(1024)} %param.10, f32[6297600]{0:T(1024)} %param.11), kind=kLoop, calls=%fused_computation.3 | loop fusion | flops 94464000 | bytes 176332800 | tf_op jit(solution)/shard_map/sub | solution.py:282
  2152.0 19.0 copy.84
  (109 shorter events, 11.4 us)
Async XLA Ops:
  7.2 313.9 %all-gather.2.cloned.1.call-start = ((), (), s32[]{:S(2)}) async-start(), calls=%async_computation.1 | async-start | bytes 37785600 | tf_op jit(solution)/shard_map/all_gather | solution.py:287
  21.7 0.7 copy-start.27
  21.7 2070.9 %all-reduce.2.cloned.1.call-start = ((), (), s32[]{:S(2)}) async-start(), calls=%async_computation.2 | async-start | bytes 50380800 | tf_op jit(solution)/shard_map/psum | solution.py:297
  22.4 373.2 %copy-start.25 = (pred[128]{0:T(512)(128)(4,1)}, pred[128]{0:T(512)(128)(4,1)S(1)}, u32[]{:S(2)}) copy-start(pred[128]{0:T(512)(128)(4,1)S(1)} %broadcast_compare_fusion.1) | copy-start | bytes 388
  359.0 9.7 copy-start.6
  367.8 14.3 copy-start.1
  369.3 13.6 copy-start.24
  375.8 10.8 copy-start.16
  382.3 4.3 copy-start.17
  382.7 1.0 copy-start.5
  383.6 9.7 copy-start.23
  386.6 1.8 copy-start.3
  387.2 6.2 slice-start.2
  388.4 5.0 slice-start.3
  393.4 1.7 copy-start.18
  395.5 4.6 slice-start
  396.6 3.5 copy-start.10
  396.6 3.5 slice-start.1
  400.0 3.1 copy-start.12
  400.1 3.4 copy-start.4
  403.4 21.4 copy-start.8
  406.8 12.1 copy-start.13
  409.8 15.0 copy-start.11
  411.2 18.3 copy-start.22
  429.5 7.0 copy-start.20
  434.9 8.6 copy-start.14
  463.6 9.3 copy-start.7
  472.8 8.4 copy-start
  478.1 7.4 slice-start.4
  481.3 4.9 slice-start.5
  1652.7 1.0 copy-start.9
  1652.7 3.6 copy-start.21
  1652.7 6.0 copy-start.2
  1652.7 6.0 copy-start.15
  1652.7 6.0 copy-start.19
  1652.7 6.0 copy-start.26
Sparse Core Ops, SparseCore 0:
  21.8 299.1 all-gather.1
  1652.8 439.6 all-reduce.1
where the time goes:
time: 2190 us; the launch traced here: 2180 us
  waiting for transfers between devices  731 us (33%)
  local copies, waits for them, and re-layouts  546 us (25%)
  other arithmetic  538 us (25%)
  blocking collectives  298 us (14%)
  matrix products  50.2 us (2%)
    unnamed x95, local copies, waits for them, and re-layouts  476 us
    psum x1, waiting for transfers between devices, on_device(): weight_grad = lax.psum(group_part, 'rep')  432 us
    all_gather x1, waiting for transfers between devices, on_device(): lax.all_gather(flat_weights.astype(jnp.bfloat16), 'shard', axis=0, tiled=...  299 us
    all_to_all x1, blocking collectives, on_device(): lax.all_to_all(local_grad.reshape(shards, owned_len), 'shard', split_axis...  298 us
    reduce_sum x1, other arithmetic, on_device(): group_part = jnp.sum(received.astype(jnp.float32), axis=0)  270 us
    all_to_all x1, other arithmetic, on_device(): lax.all_to_all(local_grad.reshape(shards, owned_len), 'shard', split_axis...  188 us
    sub x1, other arithmetic, adamw(): weights - 0.01 * (first_hat / (jnp.sqrt(second_hat) + 1e-06) + 0.01 * wei...  59.4 us
    slice x8, local copies, waits for them, and re-layouts, unpack(): lax.slice_in_dim(flat_vec, offset, offset + amount).reshape(extent)  58.2 us
  transfers between devices with their start and end apart: 2, of which 2 were waited for; matrix products, arithmetic and copies ran while one was open for 0% of the time, Pallas kernels for 0%

commit v1 on v0

--- a/solution.py
+++ b/solution.py
@@ -294,7 +294,11 @@
         local_grad.reshape(shards, owned_len), "shard", split_axis=0, concat_axis=0, tiled=True
     )
     group_part = jnp.sum(received.astype(jnp.float32), axis=0)
-    weight_grad = lax.psum(group_part, "rep")
+    weight_grad = group_part
+    for hop in (1, 2, 4, 8):
+        weight_grad = weight_grad + lax.ppermute(
+            weight_grad, "rep", [(dev, dev ^ hop) for dev in range(16)]
+        )
     new_weights, new_first, new_second = adamw(
         weight_grad, flat_weights, first_moment, second_moment
     )

time: 2190 us -> 4010 us (1.83)
  waiting for transfers between devices: 731 us -> 2490 us
  other arithmetic: 538 us -> 602 us
    ppermute x0 -> x4, waiting for transfers between devices: none -> 2200 us  [on_device(): lax.ppermute(weight_grad, 'rep', [(dev, dev ^ hop) for dev in range(16)])]
    psum x1 -> x0, waiting for transfers between devices: 432 us -> none  [on_device(): weight_grad = lax.psum(group_part, 'rep')]
    add x0 -> x3, other arithmetic: none -> 51.7 us  [on_device(): weight_grad + lax.ppermute(weight_grad, 'rep', [(dev, dev ^ hop) for dev...]
    unnamed x95 -> x102, local copies, waits for them, and re-layouts: 476 us -> 465 us
  transfers between devices with their start and end apart: 2 -> 5, of which waited for: 2 -> 5; matrix products, arithmetic and copies ran while one was open for 0% -> 0% of each run, Pallas kernels for 0% -> 0%
where the time goes in v1:
time: 4010 us; the launch traced here: 4000 us
  waiting for transfers between devices  2490 us (62%)
  other arithmetic  602 us (15%)
  local copies, waits for them, and re-layouts  535 us (13%)
  blocking collectives  298 us (7%)
  matrix products  46.9 us (1%)
    ppermute x4, waiting for transfers between devices, on_device(): lax.ppermute(weight_grad, 'rep', [(dev, dev ^ hop) for dev in range(16)])  2200 us
    unnamed x102, local copies, waits for them, and re-layouts  465 us
    all_gather x1, waiting for transfers between devices, on_device(): lax.all_gather(flat_weights.astype(jnp.bfloat16), 'shard', axis=0, tiled=...  299 us
    all_to_all x1, blocking collectives, on_device(): lax.all_to_all(local_grad.reshape(shards, owned_len), 'shard', split_axis...  298 us
    reduce_sum x1, other arithmetic, on_device(): group_part = jnp.sum(received.astype(jnp.float32), axis=0)  270 us
    all_to_all x1, other arithmetic, on_device(): lax.all_to_all(local_grad.reshape(shards, owned_len), 'shard', split_axis...  188 us
  transfers between devices with their start and end apart: 5, of which 5 were waited for; matrix products, arithmetic and copies ran while one was open for 0% of the time, Pallas kernels for 0%

profile of v1, /device:TPU:0, one launch (start us, length us, event | category | flops | bytes accessed | tf_op | source)
XLA Modules:
  0.0 3996.2 jit_solution(12158331031577133281)
XLA Ops:
  7.2 14.5 convert_element_type.203
  22.4 298.6 %all-gather.2.cloned.1.call-done = bf16[12595200]{0:T(1024)(128)(2,1)} async-done(((bf16[6297600]{0:T(1024)(128)(2,1)}), bf16[12595200]{0:T(1024)(128)(2,1)}) %all-gather.2.cloned.1.call-update) | async-done | bytes 25190416 | tf_op jit(solution)/shard_map/all_gather | solution.py:287
  321.0 11.4 fusion.43
  332.5 13.3 slice.122
  345.7 13.3 slice.119
  359.0 6.0 fusion.44
  365.0 2.8 slice.106
  369.2 4.3 slice.109
  373.5 2.0 fusion.14
  375.8 4.3 slice.112
  380.0 2.0 convolution_convert_fusion.3
  383.6 2.9 slice.114
  388.3 4.9 convolution_add_fusion
  393.4 1.5 fusion.49
  396.5 3.5 fusion.50
  400.1 3.0 multiply_reduce_fusion
  403.4 1.5 convolution_convert_fusion.1
  404.9 1.8 copy.40
  406.7 1.2 multiply_reduce_fusion.1
  407.9 1.8 fusion.8
  409.8 1.4 fusion.46
  411.1 2.2 convolution_convert_fusion
  413.4 2.5 fusion.45
  415.9 3.0 convert_bitcast_fusion.2
  418.8 5.9 convert_bitcast_fusion.1
  424.7 4.7 convert_bitcast_fusion
  430.1 2.6 copy.45
  432.7 2.2 copy.54
  434.9 1.5 constant_dynamic-update-slice_fusion.13
  437.1 2.9 copy.46
  440.0 3.6 copy.55
  444.3 2.6 copy.47
  446.9 3.5 copy.56
  450.4 3.5 copy.57
  453.9 9.6 copy.58
  463.5 9.1 copy.59
  472.8 1.5 constant_dynamic-update-slice_fusion.12
  474.3 3.8 constant_dynamic-update-slice_fusion.11
  478.1 3.2 constant_dynamic-update-slice_fusion.10
  481.3 4.2 constant_dynamic-update-slice_fusion.9
  486.1 3.6 constant_dynamic-update-slice_fusion.8
  495.0 299.9 %while.1 = (u32[]{:T(128)}, bf16[12595200]{0:T(1024)(128)(2,1)}, bf16[2,1,6297600]{2,1,0:T(2,128)(2,1)}, u32[]{}, u32[]{}) while((u32[]{:T(128)}, bf16[12595200]{0:T(1024)(128)(2,1)}, bf16[2,1,6297600]{2,1,0:T(2,128)(2,1)}, u32[]{}, u32[]{}) %tuple.55), condition=%wide.cond, body=%wide.body.sunk | while | flops 9 | bytes 62976164
  495.0 5.3 dynamic-slice.2
  500.3 144.6 %reshape_dynamic-update-slice_fusion.2 = bf16[2,1,6297600]{2,1,0:T(2,128)(2,1)} fusion(bf16[2,1,6297600]{2,1,0:T(2,128)(2,1)} %get-tuple-element.93, u32[]{:T(128)S(6)} %multiply.58, u32[]{:T(128)S(6)} %multiply.59, bf16[6297600]{0:T(1024)(128)(2,1)S(1)} %dynamic-slice.2), kind=kLoop, calls=%fused_computation.127.clone.1 | loop fusion | bytes 37785608
  644.9 5.3 dynamic-slice.2
  650.3 144.6 %reshape_dynamic-update-slice_fusion.2 = bf16[2,1,6297600]{2,1,0:T(2,128)(2,1)} fusion(bf16[2,1,6297600]{2,1,0:T(2,128)(2,1)} %get-tuple-element.93, u32[]{:T(128)S(6)} %multiply.58, u32[]{:T(128)S(6)} %multiply.59, bf16[6297600]{0:T(1024)(128)(2,1)S(1)} %dynamic-slice.2), kind=kLoop, calls=%fused_computation.127.clone.1 | loop fusion | bytes 37785608
  795.4 188.4 %reduce.3 = bf16[2,6297600]{1,0:T(2,128)(2,1)} reduce(bf16[2,1,6297600]{2,1,0:T(2,128)(2,1)} %get-tuple-element.10, bf16[]{:T(256)} %broadcast.121), dimensions={1}, to_apply=%get-tuple-element.10.reduce_sub_computation | reduce | bytes 50380800 | tf_op jit(solution)/shard_map/all_to_all | solution.py:293
  983.8 44.4 %reshape.208 = bf16[2,2,3148800]{2,1,0:T(2,128)(2,1)} reshape(bf16[2,6297600]{1,0:T(2,128)(2,1)} %reduce.3) | data formatting | bytes 50380800
  1028.2 297.9 %all_to_all.10 = bf16[2,2,3148800]{2,1,0:T(2,128)(2,1)} all-to-all(bf16[2,2,3148800]{2,1,0:T(2,128)(2,1)} %reshape.208), channel_id=1, replica_groups=mesh['rep'=16,'shard'=2] {'shard'}, dimensions={0} | all-to-all | bytes 50380800 | tf_op jit(solution)/shard_map/all_to_all | solution.py:293
  1326.1 55.6 %reshape.209 = bf16[2,1,6297600]{2,1,0:T(2,128)(2,1)} reshape(bf16[2,2,3148800]{2,1,0:T(2,128)(2,1)} %all_to_all.10) | data formatting | bytes 50380800
  1381.7 270.2 %convert_reduce_fusion = f32[6297600]{0:T(1024)} fusion(bf16[2,1,6297600]{2,1,0:T(2,128)(2,1)} %reshape.209), kind=kLoop, calls=%fused_computation | loop fusion | flops 18892800 | bytes 50380800 | tf_op jit(solution)/shard_map/reduce_sum | solution.py:296
  1651.9 37.5 collective-permute-done
  1689.4 16.0 add.160
  1705.4 1.5 collective-permute-start.1
  1707.0 541.2 %collective-permute-done.1 = f32[6297600]{0:T(1024)} collective-permute-done((f32[6297600]{0:T(1024)S(1)}, f32[6297600]{0:T(1024)}, u32[]{:S(2)}, u32[]{:S(2)}) %collective-permute-start.1) | collective-permute-done | bytes 25190432 | tf_op jit(solution)/shard_map/ppermute | solution.py:299
  2248.2 19.7 add.161
  2267.9 1.6 collective-permute-start.2
  2269.5 540.6 %collective-permute-done.2 = f32[6297600]{0:T(1024)} collective-permute-done((f32[6297600]{0:T(1024)}, f32[6297600]{0:T(1024)}, u32[]{:S(2)}, u32[]{:S(2)}) %collective-permute-start.2) | collective-permute-done | bytes 25190432 | tf_op jit(solution)/shard_map/ppermute | solution.py:299
  2810.0 16.0 add.162
  2826.0 8.9 copy-done
  2835.0 2.4 collective-permute-start.3
  2839.1 1.6 fusion.12
  2840.7 1075.9 %collective-permute-done.3 = f32[6297600]{0:T(1024)} collective-permute-done((f32[6297600]{0:T(1024)S(1)}, f32[6297600]{0:T(1024)}, u32[]{:S(2)}, u32[]{:S(2)}) %collective-permute-start.3) | collective-permute-done | bytes 25190432 | tf_op jit(solution)/shard_map/ppermute | solution.py:299
  3916.6 72.3 %multiply_subtract_fusion = (f32[6297600]{0:T(1024)}, f32[6297600]{0:T(1024)}, f32[6297600]{0:T(1024)}, f32[6297600]{0:T(1024)}) fusion(f32[6297600]{0:T(1024)} %param.9, f32[6297600]{0:T(1024)} %param.10, f32[6297600]{0:T(1024)} %param.11, f32[6297600]{0:T(1024)} %copy-done, f32[6297600]{0:T(1024)} %collective-permute-done.3), kind=kLoop, calls=%fused_computation.3 | loop fusion | flops 100761600 | bytes 226713600 | tf_op jit(solution)/shard_map/sub | solution.py:282
  (124 shorter events, 18.0 us)
Async XLA Ops:
  7.2 313.9 %all-gather.2.cloned.1.call-start = ((), (), s32[]{:S(2)}) async-start(), calls=%async_computation.1 | async-start | bytes 37785600 | tf_op jit(solution)/shard_map/all_gather | solution.py:287
  21.7 0.7 copy-start.31
  22.4 373.1 %copy-start.29 = (pred[128]{0:T(512)(128)(4,1)}, pred[128]{0:T(512)(128)(4,1)S(1)}, u32[]{:S(2)}) copy-start(pred[128]{0:T(512)(128)(4,1)S(1)} %broadcast_compare_fusion.1) | copy-start | bytes 388
  359.0 9.6 copy-start.9
  367.8 14.3 copy-start.2
  369.2 13.6 copy-start.28
  375.7 10.8 copy-start.19
  382.3 4.3 copy-start.20
  382.6 1.0 copy-start.8
  383.6 9.7 copy-start.27
  386.5 1.8 copy-start.6
  387.1 6.2 slice-start.2
  388.3 5.0 slice-start.3
  393.4 1.7 copy-start.21
  395.5 4.6 slice-start
  396.5 3.5 copy-start.13
  396.5 3.5 slice-start.1
  400.0 3.1 copy-start.15
  400.0 3.4 copy-start.7
  403.4 21.3 copy-start.11
  406.7 12.1 copy-start.16
  409.8 15.0 copy-start.14
  411.1 18.3 copy-start.25
  429.4 7.0 copy-start.23
  434.9 8.7 copy-start.17
  463.5 9.3 copy-start.10
  472.8 8.4 copy-start.1
  478.1 7.4 slice-start.4
  481.3 4.9 slice-start.5
  1651.9 37.5 collective-permute-start
  1705.4 542.7 %collective-permute-start.1 = (f32[6297600]{0:T(1024)S(1)}, f32[6297600]{0:T(1024)}, u32[]{:S(2)}, u32[]{:S(2)}) collective-permute-start(f32[6297600]{0:T(1024)S(1)} %add.160), channel_id=1, source_target_pairs={{0,4},{2,6},{4,0},{6,2},{8,12},{10,14},{12,8},{14,10},{16,20},{18,... | collective-permute-start | bytes 75571208 | tf_op jit(solution)/shard_map/ppermute | solution.py:299
  2267.8 569.5 %copy-start.4 = (bf16[1024,1024]{1,0:T(8,128)(2,1)S(1)}, bf16[1024,1024]{1,0:T(8,128)(2,1)}, u32[]{:S(2)}) copy-start(bf16[1024,1024]{1,0:T(8,128)(2,1)} %slice.109) | copy-start | bytes 6291460
  2267.8 569.5 %copy-start.12 = (f32[128,1024]{1,0:T(8,128)S(1)}, f32[128,1024]{1,0:T(8,128)}, u32[]{:S(2)}) copy-start(f32[128,1024]{1,0:T(8,128)} %copy-done.11) | copy-start | bytes 1572868
  2267.8 569.5 %copy-start.26 = (bf16[128,16,64]{0,2,1:T(8,128)(2,1)S(1)}, bf16[128,16,64]{0,2,1:T(8,128)(2,1)}, u32[]{:S(2)}) copy-start(bf16[128,16,64]{0,2,1:T(8,128)(2,1)} %copy-done.25) | copy-start | bytes 786436
  2267.8 570.4 %copy-start.5 = (bf16[1024,1024]{1,0:T(8,128)(2,1)S(1)}, bf16[1024,1024]{1,0:T(8,128)(2,1)}, u32[]{:S(2)}) copy-start(bf16[1024,1024]{1,0:T(8,128)(2,1)} %slice.112) | copy-start | bytes 6291460
  2267.9 570.4 %copy-start.24 = (bf16[16,64,128]{2,1,0:T(8,128)(2,1)S(1)}, bf16[16,64,128]{2,1,0:T(8,128)(2,1)}, u32[]{:S(2)}) copy-start(bf16[16,64,128]{2,1,0:T(8,128)(2,1)} %convolution_convert_fusion) | copy-start | bytes 786436
  2267.9 571.2 %copy-start.3 = (bf16[1024,1024]{1,0:T(8,128)(2,1)S(1)}, bf16[1024,1024]{1,0:T(8,128)(2,1)}, u32[]{:S(2)}) copy-start(bf16[1024,1024]{1,0:T(8,128)(2,1)} %copy-done.2) | copy-start | bytes 6291460
  2267.9 571.2 %copy-start.18 = (bf16[128,16,64]{0,2,1:T(8,128)(2,1)S(1)}, bf16[128,16,64]{0,2,1:T(8,128)(2,1)}, u32[]{:S(2)}) copy-start(bf16[128,16,64]{0,2,1:T(8,128)(2,1)} %get-tuple-element.49) | copy-start | bytes 786436
  2267.9 571.2 %copy-start.22 = (bf16[128,1024]{1,0:T(8,128)(2,1)S(1)}, bf16[128,1024]{1,0:T(8,128)(2,1)}, u32[]{:S(2)}) copy-start(bf16[128,1024]{1,0:T(8,128)(2,1)} %param.7) | copy-start | bytes 786436
  2267.9 571.2 %copy-start.30 = (pred[128]{0:T(512)(128)(4,1)S(1)}, pred[128]{0:T(512)(128)(4,1)}, u32[]{:S(2)}) copy-start(pred[128]{0:T(512)(128)(4,1)} %copy-done.29) | copy-start | bytes 388
  2267.9 542.1 %collective-permute-start.2 = (f32[6297600]{0:T(1024)}, f32[6297600]{0:T(1024)}, u32[]{:S(2)}, u32[]{:S(2)}) collective-permute-start(f32[6297600]{0:T(1024)} %add.161), channel_id=1, source_target_pairs={{0,8},{2,10},{4,12},{6,14},{8,0},{10,2},{12,4},{14,6},{16,24},{18,... | collective-permute-start | bytes 75571208 | tf_op jit(solution)/shard_map/ppermute | solution.py:299
  2826.0 8.9 copy-start
  2835.0 1081.6 %collective-permute-start.3 = (f32[6297600]{0:T(1024)S(1)}, f32[6297600]{0:T(1024)}, u32[]{:S(2)}, u32[]{:S(2)}) collective-permute-start(f32[6297600]{0:T(1024)S(1)} %add.162), channel_id=1, source_target_pairs={{0,16},{2,18},{4,20},{6,22},{8,24},{10,26},{12,28},{14,30},{16,0},... | collective-permute-start | bytes 75571208 | tf_op jit(solution)/shard_map/ppermute | solution.py:299
Sparse Core Ops, SparseCore 0:
  21.8 299.1 all-gather.1
